TPU v7x, 256 devices: a whole 4x4x8 slice. The times are simulated.
256 devices in a mesh: dp: 4 (over x), expert: 64 (over y, z, core).
Axes of the slice: x: 4, y: 4, z: 8, core: 2. Of those that a mesh axis runs over, the one named last changes fastest.
Arguments:
- tokens: bfloat16 [32768, 2560], P(('dp', 'expert')), may hold values from -6 to 6
- cotangent: bfloat16 [32768, 2560], P(('dp', 'expert')), may hold values from -6 to 6
- expert_ids: int32 [32768, 6], P(('dp', 'expert')), may hold values from 0 to 159, all different within a row; in each aligned block of 128 rows (0 to 127, 128 to 255, ...) at most 8 rows name the same one
- gate_weights: float32 [32768, 6], P(('dp', 'expert')), may hold values from 0.1 to 1
- gate_up: bfloat16 [64, 2, 2560, 256], P('expert', None, 'dp'), may hold values from -0.125 to 0.125
- down_proj: bfloat16 [64, 256, 2560], P('expert', None, 'dp'), may hold values from -0.1875 to 0.1875
- gate_up_first: float32 [64, 2, 2560, 256], P('expert', None, 'dp'), may hold values from -18 to 18
- gate_up_second: float32 [64, 2, 2560, 256], P('expert', None, 'dp'), may hold values from 1 to 100
- down_first: float32 [64, 256, 2560], P('expert', None, 'dp'), may hold values from -18 to 18
- down_second: float32 [64, 256, 2560], P('expert', None, 'dp'), may hold values from 1 to 100
Outputs:
- layer_out: bfloat16 [32768, 2560], P(('dp', 'expert'))
- gate_up_new: bfloat16 [64, 2, 2560, 256], P('expert', None, 'dp')
- down_new: bfloat16 [64, 256, 2560], P('expert', None, 'dp')
- gate_up_first_new: float32 [64, 2, 2560, 256], P('expert', None, 'dp')
- gate_up_second_new: float32 [64, 2, 2560, 256], P('expert', None, 'dp')
- down_first_new: float32 [64, 256, 2560], P('expert', None, 'dp')
- down_second_new: float32 [64, 256, 2560], P('expert', None, 'dp')
Inputs may be any that keep to these rules, and one draw needn't show every extreme that they name: `expert_ids`: within the 128 rows of one device no expert is named by more than 8 rows.
All inputs are finite; a program needn't handle non-finite values.
Results may differ from a plain program's by a relative error of at most 0.02.
Values may be sent and summed in bfloat16 or wider, within the bound.
A program may use at most 128 MiB of HBM per device.

v0:
```python
import functools

import jax
import jax.numpy as jnp
from jax import lax
from jax.experimental import pallas as pl
from jax.experimental.pallas import tpu as pltpu
from jax.sharding import PartitionSpec as P

TOP = 6
SPLIT = 4
CAP = 8
PAIR = 2 * CAP
NY = 4
MESH = pl.DeviceIdType.MESH

beta_one = 0.9
beta_two = 0.95
learn_rate = 0.001
decay_rate = 0.1
step_count = 10.0
epsilon = 1e-08


def adamw_update(weight, gradient, first, second):
    first_new = beta_one * first + (1.0 - beta_one) * gradient
    second_new = beta_two * second + (1.0 - beta_two) * gradient * gradient
    first_hat = first_new / (1.0 - beta_one**step_count)
    second_hat = second_new / (1.0 - beta_two**step_count)
    weight_float = weight.astype(jnp.float32)
    updated = weight_float - learn_rate * (
        first_hat / (jnp.sqrt(second_hat) + epsilon) + decay_rate * weight_float
    )
    return (updated.astype(jnp.bfloat16), first_new, second_new)


def dot(left, right):
    return jnp.dot(left, right, preferred_element_type=jnp.float32)


def chunk_of(size):
    return 512 if size % 512 == 0 else 128


def moe_kernel(
    ny,
    nz,
    tokens,
    cot,
    ids,
    gates,
    gu_own,
    dn_own,
    out,
    gpair,
    gdown,
    pack,
    comb,
    xy,
    wgu,
    wd,
    gacc,
    gs,
    part_l,
    part_r,
    from_l,
    from_r,
    zbuf,
    zrecv,
    sbuf,
    orecv,
    own_sem,
    wsend,
    wrecv,
    dsend,
    psend,
    ssend,
    near_sem,
    pair_sem,
    sib_sem,
    zsend,
    zwait,
    osend,
    owait,
    rsend,
    rwait,
    self_sem,
):
    nh = nz // 2
    experts = ny * nh
    slots = experts * CAP
    rows_t, feat = tokens.shape
    part = feat // 4
    hid = wd.shape[0]
    half, hhid = part // 2, hid // 2
    lanes = feat // 2
    batch = 4 * ny * PAIR

    g = lax.axis_index("dp")
    ei = lax.axis_index("expert")
    core = lax.rem(ei, 2)
    chip = lax.div(ei, 2)
    z = lax.rem(chip, nz)
    y = lax.div(chip, nz)
    pz = lax.rem(z, 2)
    right, left = (lax.rem(g + 1, 4), ei), (lax.rem(g + 3, 4), ei)
    sib = (g, ei + 1 - 2 * core)
    mate = (g, ei + 2 - 4 * pz)

    def device(yy, zz):
        return (g, (yy * nz + zz) * 2 + core)

    barrier = pltpu.get_barrier_semaphore()

    def greet(step, carry):
        other = lax.rem(chip + step, ny * nz)
        pl.semaphore_signal(
            barrier, inc=1, device_id=(g, other * 2 + core), device_id_type=MESH
        )
        return carry

    for who in (left, right, sib):
        pl.semaphore_signal(barrier, inc=1, device_id=who, device_id_type=MESH)
    lax.fori_loop(1, ny * nz, greet, 0)

    own_copies = [
        pltpu.make_async_copy(
            gu_own, wgu.at[:, pl.ds(pl.multiple_of(g * part, 128), part)], own_sem.at[0]
        ),
        pltpu.make_async_copy(
            dn_own, wd.at[:, pl.ds(pl.multiple_of(g * part, 128), part)], own_sem.at[1]
        ),
    ]
    for copy in own_copies:
        copy.start()

    expert_of = lax.broadcasted_iota(jnp.int32, (rows_t, slots), 1) // CAP
    place_of = lax.broadcasted_iota(jnp.int32, (rows_t, slots), 1) % CAP
    named = jnp.zeros((rows_t, slots), jnp.float32)
    weight = jnp.zeros((rows_t, slots), jnp.float32)
    for k in range(TOP):
        hit = ids[:, k : k + 1] == expert_of
        named = jnp.where(hit, 1.0, named)
        weight = jnp.where(hit, gates[:, k : k + 1], weight)
    earlier = lax.broadcasted_iota(jnp.int32, (rows_t, rows_t), 0) > lax.broadcasted_iota(
        jnp.int32, (rows_t, rows_t), 1
    )
    before = dot(
        jnp.where(earlier, 1.0, 0.0).astype(jnp.bfloat16), named.astype(jnp.bfloat16)
    )
    chosen = jnp.where(before == place_of.astype(jnp.float32), named, 0.0)
    scale = chosen * weight
    high = scale.astype(jnp.bfloat16)
    comb[0] = high
    comb[1] = (scale - high.astype(jnp.float32)).astype(jnp.bfloat16)
    pick = chosen.T.astype(jnp.bfloat16)
    slot_weight = jnp.sum(scale.T, axis=1, keepdims=True)
    kc = chunk_of(feat)
    for at in range(0, feat, kc):
        xs = dot(pick, tokens[:, at : at + kc]).reshape(experts, CAP, kc)
        ys = (dot(pick, cot[:, at : at + kc]) * slot_weight).reshape(experts, CAP, kc)
        both = jnp.concatenate([xs, ys], axis=1).reshape(experts * PAIR, kc)
        pack[:, at : at + kc] = both.astype(jnp.bfloat16)

    pl.semaphore_wait(barrier, ny * nz + 2)

    def weight_parts(owner, hf):
        return (
            wgu.at[:, pl.ds(pl.multiple_of(owner * part + hf * half, 64), half)],
            wd.at[pl.ds(hf * hhid, hhid), pl.ds(pl.multiple_of(owner * part, 128), part)],
        )

    def weight_copy(src_refs, owner, hf, lane, whom):
        return [
            pltpu.make_async_remote_copy(
                src_ref=s,
                dst_ref=d,
                send_sem=wsend.at[lane, hf, i],
                recv_sem=wrecv.at[lane, hf, i],
                device_id=whom,
                device_id_type=MESH,
            )
            for i, (s, d) in enumerate(
                zip(src_refs, weight_parts(owner, hf), strict=True)
            )
        ]

    def own_parts(hf):
        return (
            gu_own.at[:, pl.ds(hf * half, half)],
            dn_own.at[pl.ds(hf * hhid, hhid)],
        )

    g_left, g_right, g_opp = lax.rem(g + 3, 4), lax.rem(g + 1, 4), lax.rem(g + 2, 4)
    weight_sends = []
    for turn in range(2):
        for lane, whom in ((0, right), (1, left)):
            hf = turn if lane == 0 else 1 - turn
            weight_sends += weight_copy(own_parts(hf), g, hf, lane, whom)
    for copy in weight_sends:
        copy.start()

    def slot_rows(h, q, ry, count=1):
        return xy.at[pl.ds(pl.multiple_of(((h * 4 + q) * ny + ry) * PAIR, PAIR), count * PAIR)]

    def near_copy(h, ry):
        sign = 1 - 2 * lax.rem(h + pz, 2)
        zt = lax.rem(z + sign * h + nz, nz)
        yt = lax.rem(y + ry, ny)
        to = yt * nh + lax.div(zt, 2)
        return pltpu.make_async_remote_copy(
            src_ref=pack.at[pl.ds(pl.multiple_of(to * PAIR, PAIR), PAIR)],
            dst_ref=slot_rows(h, 0, ry),
            send_sem=dsend,
            recv_sem=near_sem.at[h * ny + ry],
            device_id=device(yt, zt),
            device_id_type=MESH,
        )

    mine = pltpu.make_async_copy(
        pack.at[pl.ds(pl.multiple_of(lax.div(ei, 4) * PAIR, PAIR), PAIR)],
        slot_rows(0, 0, 0),
        near_sem.at[0],
    )
    mine.start()
    for h in range(nh):
        for ry in range(ny):
            if h or ry:
                near_copy(h, ry).start()

    def hand_on(h, q, ry, whom, to_q, send_sem, recv_sem):
        return pltpu.make_async_remote_copy(
            src_ref=slot_rows(h, q, ry),
            dst_ref=slot_rows(h, to_q, ry),
            send_sem=send_sem,
            recv_sem=recv_sem,
            device_id=whom,
            device_id_type=MESH,
        )

    def arrived(ref, sem):
        pltpu.make_async_copy(ref, ref, sem).wait()

    def pass_near(h, ry):
        arrived(slot_rows(h, 0, ry), near_sem.at[h * ny + ry])
        hand_on(h, 0, ry, mate, 1, psend, pair_sem.at[h * ny + ry]).start()
        hand_on(h, 0, ry, sib, 2, ssend, sib_sem.at[h, 0]).start()

    def pass_pair(h, ry):
        arrived(slot_rows(h, 1, ry), pair_sem.at[h * ny + ry])
        hand_on(h, 1, ry, sib, 3, ssend, sib_sem.at[h, 1]).start()

    def pass_weights(lane, hf, owner, whom):
        for i, ref in enumerate(weight_parts(owner, hf)):
            arrived(ref, wrecv.at[lane, hf, i])
        copies = weight_copy(weight_parts(owner, hf), owner, hf, 2, whom)
        for copy in copies:
            copy.start()
        return copies

    gacc[...] = jnp.zeros_like(gacc)
    for h in range(nh - 1):
        for ry in range(ny):
            pass_near(h, ry)
        for ry in range(ny):
            pass_pair(h, ry)
        if h == 0:
            weight_sends += pass_weights(0, 0, g_left, right)
            weight_sends += pass_weights(1, 1, g_right, left)
    for h in range(nh - 1):
        for q in range(2):
            arrived(slot_rows(h, 2 + q, 0, ny), sib_sem.at[h, q])
    for copy in own_copies:
        copy.wait()
    for lane, hf, owner in (
        (0, 1, g_left),
        (1, 0, g_right),
        (2, 0, g_opp),
        (2, 1, g_opp),
    ):
        for i, ref in enumerate(weight_parts(owner, hf)):
            arrived(ref, wrecv.at[lane, hf, i])

    last = nh - 1

    def z_copy(h):
        return pltpu.make_async_remote_copy(
            src_ref=zbuf.at[pl.ds(pl.multiple_of(h * batch + batch // 2, PAIR), batch // 2)],
            dst_ref=zrecv.at[pl.ds(pl.multiple_of(h * (batch // 2), PAIR), batch // 2)],
            send_sem=zsend.at[h],
            recv_sem=zwait.at[h],
            device_id=sib,
            device_id_type=MESH,
        )

    def step(h, carry):
        @pl.when(h < ny)
        def _():
            pass_near(last, h)
            pass_pair(last, h)

        @pl.when(h == last)
        def _():
            for ry in range(nh, ny):
                pass_near(last, ry)
                pass_pair(last, ry)
            for q in range(2):
                arrived(slot_rows(last, 2 + q, 0, ny), sib_sem.at[last, q])

        rows = pl.ds(pl.multiple_of(h * batch, batch), batch)
        wide = (batch, hid)
        pre = jnp.zeros(wide, jnp.float32)
        up = jnp.zeros(wide, jnp.float32)
        err = jnp.zeros(wide, jnp.float32)
        for at in range(0, feat, kc):
            block = xy[rows, at : at + kc]
            pre += dot(block, wgu[0, at : at + kc])
            up += dot(block, wgu[1, at : at + kc])
            err += lax.dot_general(
                block,
                wd[:, at : at + kc],
                (((1,), (1,)), ((), ())),
                preferred_element_type=jnp.float32,
            )
        pre = pre.reshape(batch // PAIR, PAIR, hid)[:, :CAP]
        up = up.reshape(batch // PAIR, PAIR, hid)[:, :CAP]
        err = err.reshape(batch // PAIR, PAIR, hid)[:, CAP:]
        sig = jax.nn.sigmoid(pre)
        active = pre * sig * up
        d_gate = err * up * sig * (1.0 + pre * (1.0 - sig))
        d_up = err * pre * sig
        none = jnp.zeros_like(active)
        spread = jnp.concatenate(
            [
                jnp.concatenate([d_gate, d_up, none], axis=2),
                jnp.concatenate([none, none, active], axis=2),
            ],
            axis=1,
        )
        spread = spread.reshape(batch, 3 * hid).astype(jnp.bfloat16)
        for at in range(0, feat, part):
            gacc[at : at + part] += lax.dot_general(
                xy[rows, at : at + part],
                spread,
                (((0,), (0,)), ((), ())),
                preferred_element_type=jnp.float32,
            )
        act = active.reshape(batch // 2, hid).astype(jnp.bfloat16)
        kz = chunk_of(lanes) if lanes % 512 == 0 else (256 if lanes % 256 == 0 else 128)
        for at in range(0, lanes, kz):
            low = dot(act, wd[:, at : at + kz])
            top = dot(act, wd[:, lanes + at : lanes + at + kz])
            both = jnp.concatenate(
                [
                    low.reshape(batch // PAIR, CAP, kz),
                    top.reshape(batch // PAIR, CAP, kz),
                ],
                axis=1,
            )
            zbuf[rows, at : at + kz] = both.reshape(batch, kz).astype(jnp.bfloat16)
        z_copy(h).start()
        return carry

    lax.fori_loop(0, nh, step, 0)

    def grad_rows(owner, hf):
        return pl.ds(pl.multiple_of(owner * part + hf * half, 64), half)

    def grad_copy(k, src, dst, whom):
        return pltpu.make_async_remote_copy(
            src_ref=src,
            dst_ref=dst,
            send_sem=rsend.at[k],
            recv_sem=rwait.at[k],
            device_id=whom,
            device_id_type=MESH,
        )

    def gs_half(k, hf):
        return gs.at[k, pl.ds(hf * half, half)]

    def half_of(ref, hf):
        return ref.at[pl.ds(hf * half, half)]

    grad_sends = [
        grad_copy(0, gs_half(0, 0), part_l, right),
        grad_copy(1, gs_half(0, 1), part_r, left),
        grad_copy(2, gs_half(1, 1), half_of(from_l, 1), right),
        grad_copy(3, gs_half(2, 0), half_of(from_r, 0), left),
        grad_copy(4, gs_half(1, 0), half_of(from_l, 0), right),
        grad_copy(5, gs_half(2, 1), half_of(from_r, 1), left),
    ]
    for k, (slot, hf, owner) in enumerate(
        ((0, 0, g_opp), (0, 1, g_opp), (1, 1, g_right), (2, 0, g_left))
    ):
        gs[slot, hf * half : (hf + 1) * half] = gacc[grad_rows(owner, hf)].astype(
            jnp.bfloat16
        )
        grad_sends[k].start()

    def o_copy(h, q, ry):
        ys = lax.rem(y - ry + ny, ny)
        if q == 0:
            zs = lax.rem(z + (2 * pz - 1) * h + nz, nz)
        else:
            zs = lax.rem(z + (1 - 2 * pz) * (1 + h) + nz, nz)
        return pltpu.make_async_remote_copy(
            src_ref=sbuf.at[pl.ds(pl.multiple_of(((h * 2 + q) * ny + ry) * PAIR, PAIR), PAIR)],
            dst_ref=orecv.at[pl.ds(pl.multiple_of((pz * experts + lax.div(ei, 4)) * PAIR, PAIR), PAIR)],
            send_sem=osend,
            recv_sem=owait,
            device_id=device(ys, zs),
            device_id_type=MESH,
        )

    for h in range(nh):
        z_copy(h).wait_recv()
        a, b = h * batch, h * (batch // 2)
        total = zbuf[a : a + batch // 2].astype(jnp.float32) + zrecv[
            b : b + batch // 2
        ].astype(jnp.float32)
        sbuf[b : b + batch // 2] = total.astype(jnp.bfloat16)
        for q in range(2):
            for ry in range(ny):
                if h or q or ry:
                    o_copy(h, q, ry).start()
                else:
                    pltpu.make_async_copy(
                        sbuf.at[pl.ds(0, PAIR)],
                        orecv.at[pl.ds(pl.multiple_of((pz * experts + lax.div(ei, 4)) * PAIR, PAIR), PAIR)],
                        owait,
                    ).start()

    for k, (came, slot, hf, owner) in enumerate(
        ((part_l, 1, 0, g_right), (part_r, 2, 1, g_left))
    ):
        arrived(came, rwait.at[k])
        gs[slot, hf * half : (hf + 1) * half] = (
            gacc[grad_rows(owner, hf)] + came[...].astype(jnp.float32)
        ).astype(jnp.bfloat16)
        grad_sends[4 + k].start()

    arrived(orecv, owait)
    for side in range(2):
        done = jnp.zeros((rows_t, lanes), jnp.float32)
        for which in range(2):
            part_o = orecv[which * experts * PAIR : (which + 1) * experts * PAIR]
            part_o = part_o.astype(jnp.float32).reshape(experts, PAIR, lanes)
            part_o = part_o[:, side * CAP : (side + 1) * CAP].reshape(slots, lanes)
            part_o = part_o.astype(jnp.bfloat16)
            done += dot(comb[0], part_o) + dot(comb[1], part_o)
        out[:, side * lanes : (side + 1) * lanes] = done.astype(jnp.bfloat16)

    for first, second, hf in ((3, 4, 0), (2, 5, 1)):
        for k in (first, second):
            dst = half_of(from_l if k in (2, 4) else from_r, hf)
            arrived(dst, rwait.at[k])
        at = hf * half
        total = (
            gacc[grad_rows(g, hf)]
            + from_l[at : at + half].astype(jnp.float32)
            + from_r[at : at + half].astype(jnp.float32)
        )
        gpair[0, at : at + half] = total[:, :hid]
        gpair[1, at : at + half] = total[:, hid : 2 * hid]
        gdown[at : at + half] = total[:, 2 * hid :]

    for copy in weight_sends + grad_sends:
        copy.wait_send()
    for h in range(nh):
        z_copy(h).wait_send()
    count = nh * ny
    arrived(xy.at[pl.ds(0, (count - 1) * PAIR)], dsend)
    arrived(xy.at[pl.ds(0, count * PAIR)], psend)
    arrived(xy.at[pl.ds(0, 2 * count * PAIR)], ssend)
    arrived(sbuf.at[pl.ds(0, (2 * count - 1) * PAIR)], osend)


def experts_step(tokens, cotangent, expert_ids, gate_weights, pair_own, down_own):
    shards = lax.axis_size("expert")
    ny, nz = NY, shards // (2 * NY)
    nh = nz // 2
    experts = shards // SPLIT
    rows, feat = tokens.shape
    hid = down_own.shape[0]
    part, lanes = feat // 4, feat // 2
    slots = experts * CAP
    batch = 4 * ny * PAIR
    vmem = pl.BlockSpec(memory_space=pltpu.VMEM)
    hbm = pl.BlockSpec(memory_space=pl.ANY)
    bf, f32 = jnp.bfloat16, jnp.float32
    dma = pltpu.SemaphoreType.DMA
    return pl.pallas_call(
        functools.partial(moe_kernel, ny, nz),
        out_shape=(
            jax.ShapeDtypeStruct((rows, feat), bf),
            jax.ShapeDtypeStruct((2, part, hid), f32),
            jax.ShapeDtypeStruct((part, hid), f32),
        ),
        in_specs=[vmem, vmem, vmem, vmem, hbm, hbm],
        out_specs=(vmem, vmem, vmem),
        scratch_shapes=[
            pltpu.VMEM((experts * PAIR, feat), bf),
            pltpu.VMEM((2, rows, slots), bf),
            pltpu.VMEM((nh * batch, feat), bf),
            pltpu.VMEM((2, feat, hid), bf),
            pltpu.VMEM((hid, feat), bf),
            pltpu.VMEM((feat, 3 * hid), f32),
            pltpu.VMEM((3, part, 3 * hid), bf),
            pltpu.VMEM((part // 2, 3 * hid), bf),
            pltpu.VMEM((part // 2, 3 * hid), bf),
            pltpu.VMEM((part, 3 * hid), bf),
            pltpu.VMEM((part, 3 * hid), bf),
            pltpu.VMEM((nh * batch, lanes), bf),
            pltpu.VMEM((nh * batch // 2, lanes), bf),
            pltpu.VMEM((nh * batch // 2, lanes), bf),
            pltpu.VMEM((2 * experts * PAIR, lanes), bf),
            dma((2,)),
            dma((3, 2, 2)),
            dma((3, 2, 2)),
            dma,
            dma,
            dma,
            dma((nh * ny,)),
            dma((nh * ny,)),
            dma((nh, 2)),
            dma((nh,)),
            dma((nh,)),
            dma,
            dma,
            dma((6,)),
            dma((6,)),
            dma,
        ],
        compiler_params=pltpu.CompilerParams(
            collective_id=0,
            has_side_effects=True,
            vmem_limit_bytes=60 * 1024 * 1024,
        ),
        cost_estimate=pl.CostEstimate(
            flops=8_000_000_000, bytes_accessed=10_000_000, transcendentals=200_000
        ),
    )(tokens, cotangent, expert_ids, gate_weights, pair_own, down_own)


def body(
    tokens,
    cotangent,
    expert_ids,
    gate_weights,
    gate_up,
    down_proj,
    gate_up_first,
    gate_up_second,
    down_first,
    down_second,
):
    layer_out, own_pair, own_down = experts_step(
        tokens, cotangent, expert_ids, gate_weights, gate_up[0], down_proj[0]
    )
    gate_up_new, gate_up_first_new, gate_up_second_new = adamw_update(
        gate_up, own_pair[None], gate_up_first, gate_up_second
    )
    down_new, down_first_new, down_second_new = adamw_update(
        down_proj, own_down.T[None], down_first, down_second
    )
    return (
        layer_out,
        gate_up_new,
        down_new,
        gate_up_first_new,
        gate_up_second_new,
        down_first_new,
        down_second_new,
    )


def solution(mesh):
    return jax.shard_map(
        body,
        mesh=mesh,
        in_specs=(
            P(("dp", "expert"), None),
            P(("dp", "expert"), None),
            P(("dp", "expert"), None),
            P(("dp", "expert"), None),
            P("expert", None, "dp", None),
            P("expert", None, "dp"),
            P("expert", None, "dp", None),
            P("expert", None, "dp", None),
            P("expert", None, "dp"),
            P("expert", None, "dp"),
        ),
        out_specs=(
            P(("dp", "expert"), None),
            P("expert", None, "dp", None),
            P("expert", None, "dp"),
            P("expert", None, "dp", None),
            P("expert", None, "dp", None),
            P("expert", None, "dp"),
            P("expert", None, "dp"),
        ),
        check_vma=False,
    )
```

profile of v0, /device:TPU:32, one launch (start us, length us, event | category | flops | bytes accessed | tf_op | source)
XLA Modules:
  0.0 129.1 jit_solution(3653087558410854221)
XLA Ops:
  0.6 1.4 %copy.17.ids = s32[128,6]{1,0:T(8,128)} copy(s32[128,6]{0,1:T(8,128)} %param.12) | data formatting | bytes 6144 | tf_op args[2]
  2.1 1.4 %copy.18.gates = f32[128,6]{1,0:T(8,128)} copy(f32[128,6]{0,1:T(8,128)} %param.13) | data formatting | bytes 6144 | tf_op args[3]
  3.5 0.0 copy-start
  3.5 0.0 copy-start.1
  3.5 114.3 %shard_map.153 = (bf16[128,2560]{1,0:T(8,128)(2,1)}, f32[2,640,256]{2,1,0:T(8,128)}, f32[640,256]{1,0:T(8,128)}) custom-call(bf16[128,2560]{1,0:T(8,128)(2,1)} %tokens.1, bf16[128,2560]{1,0:T(8,128)(2,1)} %cot.1, s32[128,6]{1,0:T(8,128)} %copy.17.ids, f32[128,6]{1,0:T(8,128)} %copy.18.gates, bf16[2,640,256]{2,1,0:T(8,128)(2,1)} %bitcast.25, ...), custom_call_target="tpu_custom_call" | custom-call | flops 8000000000 | bytes 10000000 | tf_op jit(solution)/shard_map/pallas_call | solution.py:493
  117.8 0.0 copy-done
  117.8 0.0 copy-done.1
  117.8 0.0 copy-start.2
  117.8 4.1 %fusion.2 = (bf16[1,2,640,256]{3,2,1,0:T(8,128)(2,1)}, f32[1,2,640,256]{3,2,1,0:T(8,128)}, f32[1,2,640,256]{3,2,1,0:T(8,128)}) fusion(bf16[1,2,640,256]{3,2,1,0:T(8,128)(2,1)} %param.14, f32[2,640,256]{2,1,0:T(8,128)} %get-tuple-element.11, f32[1,2,640,256]{3,2,1,0:T(8,128)S(1)} %copy-done, f32[1,2,640,256]{3,2,1,0:T(8,128)S(1)} %copy-done.1), kind=kLoop, calls=%fused_computation.5 | loop fusion | flops 5570560 | bytes 7864320 | tf_op jit(solution)/shard_map/convert_element_type | solution.py:34
  121.9 0.0 copy-start.3
  121.9 1.2 copy.19
  123.1 0.0 copy-done.2
  123.1 0.2 copy.20
  123.3 0.0 copy-done.3
  123.4 0.2 copy.21
  123.6 1.7 %fusion.7 = (bf16[1,256,640]{1,2,0:T(8,128)(2,1)S(1)}, f32[1,256,640]{1,2,0:T(8,128)S(1)}, f32[1,256,640]{1,2,0:T(8,128)S(1)}) fusion(bf16[1,256,640]{1,2,0:T(8,128)(2,1)S(1)} %copy.19, f32[640,256]{1,0:T(8,128)} %get-tuple-element.12, f32[1,256,640]{1,2,0:T(8,128)S(1)} %copy.20, f32[1,256,640]{1,2,0:T(8,128)S(1)} %copy.21), kind=kLoop, calls=%fused_computation.14 | loop fusion | flops 2785280 | bytes 3932160 | tf_op jit(solution)/shard_map/convert_element_type | solution.py:34
  125.3 0.9 copy.22
  126.2 0.0 copy-start.4
  126.2 1.1 copy.23
  127.2 1.1 copy.24
  128.3 0.0 copy-done.4
  128.3 0.8 copy.26
Async XLA Ops:
  3.5 114.3 %copy-start = (f32[1,2,640,256]{3,2,1,0:T(8,128)S(1)}, f32[1,2,640,256]{3,2,1,0:T(8,128)}, u32[]{:S(2)}) copy-start(f32[1,2,640,256]{3,2,1,0:T(8,128)} %param.16) | copy-start | bytes 3932164
  3.5 114.3 %copy-start.1 = (f32[1,2,640,256]{3,2,1,0:T(8,128)S(1)}, f32[1,2,640,256]{3,2,1,0:T(8,128)}, u32[]{:S(2)}) copy-start(f32[1,2,640,256]{3,2,1,0:T(8,128)} %param.17) | copy-start | bytes 3932164
  117.8 5.3 %copy-start.2 = (f32[1,256,640]{2,1,0:T(8,128)S(1)}, f32[1,256,640]{2,1,0:T(8,128)}, u32[]{:S(2)}) copy-start(f32[1,256,640]{2,1,0:T(8,128)} %param.18) | copy-start | bytes 1966084
  121.9 1.5 %copy-start.3 = (f32[1,256,640]{2,1,0:T(8,128)S(1)}, f32[1,256,640]{2,1,0:T(8,128)}, u32[]{:S(2)}) copy-start(f32[1,256,640]{2,1,0:T(8,128)} %param.19) | copy-start | bytes 1966084
  126.2 2.1 %copy-start.4 = (bf16[128,2560]{1,0:T(8,128)(2,1)S(1)}, bf16[128,2560]{1,0:T(8,128)(2,1)}, u32[]{:S(2)}) copy-start(bf16[128,2560]{1,0:T(8,128)(2,1)} %get-tuple-element.33) | copy-start | bytes 1966084
where the time goes:
time: 130 us; the launch traced here: 129 us
  Pallas kernels  114 us (88%)
  local copies, waits for them, and re-layouts  8.41 us (6%)
  other arithmetic  5.72 us (4%)
    pallas_call x1, Pallas kernels, experts_step(): pl.pallas_call(functools.partial(moe_kernel, ny, nz), out_shape=(jax.Shap...  114 us
    unnamed x19, local copies, waits for them, and re-layouts  8.41 us
    convert_element_type x2, other arithmetic, adamw_update(): return (updated.astype(jnp.bfloat16), first_new, second_new)  5.72 us

commit v1 on v0

--- a/solution.py
+++ b/solution.py
@@ -45,15 +45,19 @@
 def moe_kernel(
     ny,
     nz,
-    tokens,
-    cot,
-    ids,
-    gates,
+    tokens_in,
+    cot_in,
+    ids_in,
+    gates_in,
     gu_own,
     dn_own,
     out,
     gpair,
     gdown,
+    tokens,
+    cot,
+    ids,
+    gates,
     pack,
     comb,
     xy,
@@ -84,7 +88,7 @@
     owait,
     rsend,
     rwait,
-    self_sem,
+    in_sem,
 ):
     nh = nz // 2
     experts = ny * nh
@@ -110,6 +114,15 @@
     def device(yy, zz):
         return (g, (yy * nz + zz) * 2 + core)
 
+    loads = [
+        pltpu.make_async_copy(src, dst, in_sem.at[i])
+        for i, (src, dst) in enumerate(
+            ((ids_in, ids), (gates_in, gates), (tokens_in, tokens), (cot_in, cot))
+        )
+    ]
+    for copy in loads:
+        copy.start()
+
     barrier = pltpu.get_barrier_semaphore()
 
     def greet(step, carry):
@@ -133,34 +146,38 @@
     ]
     for copy in own_copies:
         copy.start()
-
-    expert_of = lax.broadcasted_iota(jnp.int32, (rows_t, slots), 1) // CAP
-    place_of = lax.broadcasted_iota(jnp.int32, (rows_t, slots), 1) % CAP
-    named = jnp.zeros((rows_t, slots), jnp.float32)
-    weight = jnp.zeros((rows_t, slots), jnp.float32)
+    for copy in loads:
+        copy.wait()
+
+    row = lax.broadcasted_iota(jnp.int32, (slots, rows_t), 0)
+    named = jnp.zeros((slots, rows_t), jnp.float32)
+    weight = jnp.zeros((slots, rows_t), jnp.float32)
     for k in range(TOP):
-        hit = ids[:, k : k + 1] == expert_of
+        hit = ids[k : k + 1] == row // CAP
         named = jnp.where(hit, 1.0, named)
-        weight = jnp.where(hit, gates[:, k : k + 1], weight)
-    earlier = lax.broadcasted_iota(jnp.int32, (rows_t, rows_t), 0) > lax.broadcasted_iota(
+        weight = jnp.where(hit, gates[k : k + 1], weight)
+    earlier = lax.broadcasted_iota(jnp.int32, (rows_t, rows_t), 0) < lax.broadcasted_iota(
         jnp.int32, (rows_t, rows_t), 1
     )
     before = dot(
-        jnp.where(earlier, 1.0, 0.0).astype(jnp.bfloat16), named.astype(jnp.bfloat16)
-    )
-    chosen = jnp.where(before == place_of.astype(jnp.float32), named, 0.0)
+        named.astype(jnp.bfloat16), jnp.where(earlier, 1.0, 0.0).astype(jnp.bfloat16)
+    )
+    chosen = jnp.where(before == (row % CAP).astype(jnp.float32), named, 0.0)
     scale = chosen * weight
-    high = scale.astype(jnp.bfloat16)
+    pick = chosen.astype(jnp.bfloat16)
+    slot_weight = jnp.sum(scale, axis=1, keepdims=True)
+    back = scale.T
+    high = back.astype(jnp.bfloat16)
     comb[0] = high
-    comb[1] = (scale - high.astype(jnp.float32)).astype(jnp.bfloat16)
-    pick = chosen.T.astype(jnp.bfloat16)
-    slot_weight = jnp.sum(scale.T, axis=1, keepdims=True)
+    comb[1] = (back - high.astype(jnp.float32)).astype(jnp.bfloat16)
     kc = chunk_of(feat)
     for at in range(0, feat, kc):
         xs = dot(pick, tokens[:, at : at + kc]).reshape(experts, CAP, kc)
         ys = (dot(pick, cot[:, at : at + kc]) * slot_weight).reshape(experts, CAP, kc)
         both = jnp.concatenate([xs, ys], axis=1).reshape(experts * PAIR, kc)
         pack[:, at : at + kc] = both.astype(jnp.bfloat16)
+
+    gacc[...] = jnp.zeros_like(gacc)
 
     pl.semaphore_wait(barrier, ny * nz + 2)
 
@@ -223,7 +240,7 @@
         near_sem.at[0],
     )
     mine.start()
-    for h in range(nh):
+    for h in range(min(nh, 3)):
         for ry in range(ny):
             if h or ry:
                 near_copy(h, ry).start()
@@ -258,16 +275,20 @@
             copy.start()
         return copies
 
-    gacc[...] = jnp.zeros_like(gacc)
-    for h in range(nh - 1):
+    last = nh - 1
+    for h in range(nh):
         for ry in range(ny):
             pass_near(h, ry)
-        for ry in range(ny):
-            pass_pair(h, ry)
-        if h == 0:
+        if 3 <= h + 2 < nh:
+            for ry in range(ny):
+                near_copy(h + 2, ry).start()
+        if h:
+            for ry in range(ny):
+                pass_pair(h - 1, ry)
+        if h == min(2, last):
             weight_sends += pass_weights(0, 0, g_left, right)
             weight_sends += pass_weights(1, 1, g_right, left)
-    for h in range(nh - 1):
+    for h in range(last):
         for q in range(2):
             arrived(slot_rows(h, 2 + q, 0, ny), sib_sem.at[h, q])
     for copy in own_copies:
@@ -281,8 +302,6 @@
         for i, ref in enumerate(weight_parts(owner, hf)):
             arrived(ref, wrecv.at[lane, hf, i])
 
-    last = nh - 1
-
     def z_copy(h):
         return pltpu.make_async_remote_copy(
             src_ref=zbuf.at[pl.ds(pl.multiple_of(h * batch + batch // 2, PAIR), batch // 2)],
@@ -293,25 +312,14 @@
             device_id_type=MESH,
         )
 
-    def step(h, carry):
-        @pl.when(h < ny)
-        def _():
-            pass_near(last, h)
-            pass_pair(last, h)
-
-        @pl.when(h == last)
-        def _():
-            for ry in range(nh, ny):
-                pass_near(last, ry)
-                pass_pair(last, ry)
-            for q in range(2):
-                arrived(slot_rows(last, 2 + q, 0, ny), sib_sem.at[last, q])
-
-        rows = pl.ds(pl.multiple_of(h * batch, batch), batch)
-        wide = (batch, hid)
-        pre = jnp.zeros(wide, jnp.float32)
-        up = jnp.zeros(wide, jnp.float32)
-        err = jnp.zeros(wide, jnp.float32)
+    def rows_of(h):
+        return pl.ds(pl.multiple_of(h * batch, batch), batch)
+
+    def activations(h):
+        rows = rows_of(h)
+        pre = jnp.zeros((batch, hid), jnp.float32)
+        up = jnp.zeros((batch, hid), jnp.float32)
+        err = jnp.zeros((batch, hid), jnp.float32)
         for at in range(0, feat, kc):
             block = xy[rows, at : at + kc]
             pre += dot(block, wgu[0, at : at + kc])
@@ -338,15 +346,19 @@
             axis=1,
         )
         spread = spread.reshape(batch, 3 * hid).astype(jnp.bfloat16)
-        for at in range(0, feat, part):
-            gacc[at : at + part] += lax.dot_general(
-                xy[rows, at : at + part],
-                spread,
-                (((0,), (0,)), ((), ())),
-                preferred_element_type=jnp.float32,
-            )
-        act = active.reshape(batch // 2, hid).astype(jnp.bfloat16)
-        kz = chunk_of(lanes) if lanes % 512 == 0 else (256 if lanes % 256 == 0 else 128)
+        return spread, active.reshape(batch // 2, hid).astype(jnp.bfloat16)
+
+    def weight_grad(h, owner, spread):
+        at = pl.ds(pl.multiple_of(owner * part, 128), part)
+        return gacc[at] + lax.dot_general(
+            xy[rows_of(h), at],
+            spread,
+            (((0,), (0,)), ((), ())),
+            preferred_element_type=jnp.float32,
+        )
+
+    def project(h, act):
+        kz = 256 if lanes % 256 == 0 else 128
         for at in range(0, lanes, kz):
             low = dot(act, wd[:, at : at + kz])
             top = dot(act, wd[:, lanes + at : lanes + at + kz])
@@ -357,14 +369,30 @@
                 ],
                 axis=1,
             )
-            zbuf[rows, at : at + kz] = both.reshape(batch, kz).astype(jnp.bfloat16)
+            zbuf[rows_of(h), at : at + kz] = both.reshape(batch, kz).astype(jnp.bfloat16)
         z_copy(h).start()
+
+    each = -(-ny // max(1, last - 1))
+
+    def step(h, carry):
+        spread, act = activations(h)
+        for owner in range(4):
+            gacc[owner * part : (owner + 1) * part] = weight_grad(h, owner, spread)
+        project(h, act)
+        for ry in range(ny):
+
+            @pl.when(h == ry // each)
+            def _(ry=ry):
+                pass_pair(last, ry)
+
         return carry
 
-    lax.fori_loop(0, nh, step, 0)
-
-    def grad_rows(owner, hf):
-        return pl.ds(pl.multiple_of(owner * part + hf * half, 64), half)
+    lax.fori_loop(0, last, step, 0)
+    for q in range(2):
+        arrived(slot_rows(last, 2 + q, 0, ny), sib_sem.at[last, q])
+
+    def own_rows(owner):
+        return pl.ds(pl.multiple_of(owner * part, 128), part)
 
     def grad_copy(k, src, dst, whom):
         return pltpu.make_async_remote_copy(
@@ -376,27 +404,26 @@
             device_id_type=MESH,
         )
 
-    def gs_half(k, hf):
-        return gs.at[k, pl.ds(hf * half, half)]
-
-    def half_of(ref, hf):
-        return ref.at[pl.ds(hf * half, half)]
-
     grad_sends = [
-        grad_copy(0, gs_half(0, 0), part_l, right),
-        grad_copy(1, gs_half(0, 1), part_r, left),
-        grad_copy(2, gs_half(1, 1), half_of(from_l, 1), right),
-        grad_copy(3, gs_half(2, 0), half_of(from_r, 0), left),
-        grad_copy(4, gs_half(1, 0), half_of(from_l, 0), right),
-        grad_copy(5, gs_half(2, 1), half_of(from_r, 1), left),
+        grad_copy(0, gs.at[0, 0], part_l, right),
+        grad_copy(1, gs.at[0, 1], part_r, left),
+        grad_copy(2, gs.at[1, 1], from_l.at[1], right),
+        grad_copy(3, gs.at[2, 0], from_r.at[0], left),
+        grad_copy(4, gs.at[1, 0], from_l.at[0], right),
+        grad_copy(5, gs.at[2, 1], from_r.at[1], left),
     ]
-    for k, (slot, hf, owner) in enumerate(
-        ((0, 0, g_opp), (0, 1, g_opp), (1, 1, g_right), (2, 0, g_left))
-    ):
-        gs[slot, hf * half : (hf + 1) * half] = gacc[grad_rows(owner, hf)].astype(
-            jnp.bfloat16
-        )
-        grad_sends[k].start()
+    spread, act = activations(last)
+    wide = gacc.shape[1] // 2
+    for slot, owner, sent in ((0, g_opp, ((0, 0), (1, 1))), (1, g_right, ((2, 1),)), (2, g_left, ((3, 0),))):
+        full = weight_grad(last, owner, spread)
+        for k, hf in sent:
+            gs[slot, hf] = full[:, hf * wide : (hf + 1) * wide].astype(jnp.bfloat16)
+            grad_sends[k].start()
+        if slot:
+            hf = 1 - sent[0][1]
+            gacc[own_rows(owner), hf * wide : (hf + 1) * wide] = full[
+                :, hf * wide : (hf + 1) * wide
+            ]
 
     def o_copy(h, q, ry):
         ys = lax.rem(y - ry + ny, ny)
@@ -413,7 +440,11 @@
             device_id_type=MESH,
         )
 
-    for h in range(nh):
+    here = pl.ds(
+        pl.multiple_of((pz * experts + lax.div(ei, 4)) * PAIR, PAIR), PAIR
+    )
+
+    def send_back(h):
         z_copy(h).wait_recv()
         a, b = h * batch, h * (batch // 2)
         total = zbuf[a : a + batch // 2].astype(jnp.float32) + zrecv[
@@ -426,17 +457,22 @@
                     o_copy(h, q, ry).start()
                 else:
                     pltpu.make_async_copy(
-                        sbuf.at[pl.ds(0, PAIR)],
-                        orecv.at[pl.ds(pl.multiple_of((pz * experts + lax.div(ei, 4)) * PAIR, PAIR), PAIR)],
-                        owait,
+                        sbuf.at[pl.ds(0, PAIR)], orecv.at[here], owait
                     ).start()
+
+    project(last, act)
+    for h in range(last):
+        send_back(h)
+    gacc[own_rows(g)] = weight_grad(last, g, spread)
+    send_back(last)
 
     for k, (came, slot, hf, owner) in enumerate(
         ((part_l, 1, 0, g_right), (part_r, 2, 1, g_left))
     ):
         arrived(came, rwait.at[k])
-        gs[slot, hf * half : (hf + 1) * half] = (
-            gacc[grad_rows(owner, hf)] + came[...].astype(jnp.float32)
+        gs[slot, hf] = (
+            gacc[own_rows(owner), hf * wide : (hf + 1) * wide]
+            + came[...].astype(jnp.float32)
         ).astype(jnp.bfloat16)
         grad_sends[4 + k].start()
 
@@ -451,19 +487,19 @@
             done += dot(comb[0], part_o) + dot(comb[1], part_o)
         out[:, side * lanes : (side + 1) * lanes] = done.astype(jnp.bfloat16)
 
-    for first, second, hf in ((3, 4, 0), (2, 5, 1)):
-        for k in (first, second):
-            dst = half_of(from_l if k in (2, 4) else from_r, hf)
-            arrived(dst, rwait.at[k])
-        at = hf * half
-        total = (
-            gacc[grad_rows(g, hf)]
-            + from_l[at : at + half].astype(jnp.float32)
-            + from_r[at : at + half].astype(jnp.float32)
-        )
-        gpair[0, at : at + half] = total[:, :hid]
-        gpair[1, at : at + half] = total[:, hid : 2 * hid]
-        gdown[at : at + half] = total[:, 2 * hid :]
+    totals = []
+    for first, second, hf in ((4, 3, 0), (2, 5, 1)):
+        arrived(from_l.at[hf], rwait.at[first])
+        arrived(from_r.at[hf], rwait.at[second])
+        totals.append(
+            gacc[own_rows(g), hf * wide : (hf + 1) * wide]
+            + from_l[hf].astype(jnp.float32)
+            + from_r[hf].astype(jnp.float32)
+        )
+    gpair[0] = totals[0][:, :hid]
+    gpair[1, :, : hid // 2] = totals[0][:, hid:]
+    gpair[1, :, hid // 2 :] = totals[1][:, : hid // 2]
+    gdown[...] = totals[1][:, hid // 2 :].T
 
     for copy in weight_sends + grad_sends:
         copy.wait_send()
@@ -483,11 +519,11 @@
     experts = shards // SPLIT
     rows, feat = tokens.shape
     hid = down_own.shape[0]
-    part, lanes = feat // 4, feat // 2
+    part, lanes, wide = feat // 4, feat // 2, 3 * hid // 2
     slots = experts * CAP
     batch = 4 * ny * PAIR
     vmem = pl.BlockSpec(memory_space=pltpu.VMEM)
-    hbm = pl.BlockSpec(memory_space=pl.ANY)
+    hbm = pl.BlockSpec(memory_space=pltpu.HBM)
     bf, f32 = jnp.bfloat16, jnp.float32
     dma = pltpu.SemaphoreType.DMA
     return pl.pallas_call(
@@ -495,22 +531,26 @@
         out_shape=(
             jax.ShapeDtypeStruct((rows, feat), bf),
             jax.ShapeDtypeStruct((2, part, hid), f32),
-            jax.ShapeDtypeStruct((part, hid), f32),
+            jax.ShapeDtypeStruct((hid, part), f32),
         ),
-        in_specs=[vmem, vmem, vmem, vmem, hbm, hbm],
+        in_specs=[hbm] * 6,
         out_specs=(vmem, vmem, vmem),
         scratch_shapes=[
+            pltpu.VMEM((rows, feat), bf),
+            pltpu.VMEM((rows, feat), bf),
+            pltpu.VMEM((TOP, rows), jnp.int32),
+            pltpu.VMEM((TOP, rows), f32),
             pltpu.VMEM((experts * PAIR, feat), bf),
             pltpu.VMEM((2, rows, slots), bf),
             pltpu.VMEM((nh * batch, feat), bf),
             pltpu.VMEM((2, feat, hid), bf),
             pltpu.VMEM((hid, feat), bf),
             pltpu.VMEM((feat, 3 * hid), f32),
-            pltpu.VMEM((3, part, 3 * hid), bf),
-            pltpu.VMEM((part // 2, 3 * hid), bf),
-            pltpu.VMEM((part // 2, 3 * hid), bf),
-            pltpu.VMEM((part, 3 * hid), bf),
-            pltpu.VMEM((part, 3 * hid), bf),
+            pltpu.VMEM((3, 2, part, wide), bf),
+            pltpu.VMEM((part, wide), bf),
+            pltpu.VMEM((part, wide), bf),
+            pltpu.VMEM((2, part, wide), bf),
+            pltpu.VMEM((2, part, wide), bf),
             pltpu.VMEM((nh * batch, lanes), bf),
             pltpu.VMEM((nh * batch // 2, lanes), bf),
             pltpu.VMEM((nh * batch // 2, lanes), bf),
@@ -530,17 +570,29 @@
             dma,
             dma((6,)),
             dma((6,)),
-            dma,
+            dma((4,)),
         ],
         compiler_params=pltpu.CompilerParams(
             collective_id=0,
             has_side_effects=True,
-            vmem_limit_bytes=60 * 1024 * 1024,
+            vmem_limit_bytes=46 * 1024 * 1024,
         ),
         cost_estimate=pl.CostEstimate(
             flops=8_000_000_000, bytes_accessed=10_000_000, transcendentals=200_000
         ),
-    )(tokens, cotangent, expert_ids, gate_weights, pair_own, down_own)
+    )(
+        *(
+            pltpu.with_memory_space_constraint(a, pltpu.HBM)
+            for a in (
+                tokens,
+                cotangent,
+                expert_ids.T,
+                gate_weights.T,
+                pair_own,
+                down_own,
+            )
+        )
+    )
 
 
 def body(
@@ -562,7 +614,7 @@
         gate_up, own_pair[None], gate_up_first, gate_up_second
     )
     down_new, down_first_new, down_second_new = adamw_update(
-        down_proj, own_down.T[None], down_first, down_second
+        down_proj, own_down[None], down_first, down_second
     )
     return (
         layer_out,

time: 130 us -> 104 us (0.80)
  Pallas kernels: 114 us -> 98.3 us
  local copies, waits for them, and re-layouts: 8.41 us -> 0.87 us
  other arithmetic: 5.72 us -> 4.04 us
    pallas_call x1, Pallas kernels: 114 us -> 98.3 us  [experts_step(): pl.pallas_call(functools.partial(moe_kernel, ny, nz), out_shape=(jax.Shap...]
    unnamed x19 -> x13, local copies, waits for them, and re-layouts: 8.41 us -> 0.87 us
    convert_element_type x2, other arithmetic: 5.72 us -> 4.04 us  [adamw_update(): return (updated.astype(jnp.bfloat16), first_new, second_new)]
where the time goes in v1:
time: 104 us
  Pallas kernels  98.3 us (95%)
  other arithmetic  4.04 us (4%)
    pallas_call x1, Pallas kernels, experts_step(): pl.pallas_call(functools.partial(moe_kernel, ny, nz), out_shape=(jax.Shap...  98.3 us
    convert_element_type x2, other arithmetic, adamw_update(): return (updated.astype(jnp.bfloat16), first_new, second_new)  4.04 us

profile of v1, /device:TPU:32, one launch (start us, length us, event | category | flops | bytes accessed | tf_op | source)
XLA Modules:
  0.0 104.0 jit_solution(2154890146641804705)
XLA Ops:
  0.6 0.0 copy-start
  0.6 0.0 copy-start.1
  0.7 0.0 copy-start.2
  0.7 98.3 %shard_map.153 = (bf16[128,2560]{1,0:T(8,128)(2,1)S(1)}, f32[2,640,256]{2,1,0:T(8,128)S(1)}, f32[256,640]{1,0:T(8,128)S(1)}) custom-call(bf16[128,2560]{1,0:T(8,128)(2,1)} %tokens_in.1, bf16[128,2560]{1,0:T(8,128)(2,1)} %cot_in.1, s32[6,128]{1,0:T(8,128)} %bitcast.22, f32[6,128]{1,0:T(8,128)} %bitcast.23, bf16[2,640,256]{2,1,0:T(8,128)(2,1)} %bitcast.20, ...), custom_call_target="tpu_custom_call" | custom-call | flops 8000000000 | bytes 10000000 | tf_op jit(solution)/shard_map/pallas_call | solution.py:529
  99.0 0.0 copy-done
  99.0 0.0 copy-done.1
  99.0 0.0 copy-done.2
  99.0 0.0 copy-start.3
  99.1 0.0 copy-start.4
  99.1 0.0 copy-start.5
  99.1 2.5 %fusion.2 = (bf16[1,2,640,256]{3,2,1,0:T(8,128)(2,1)}, f32[1,2,640,256]{3,2,1,0:T(8,128)}, f32[1,2,640,256]{3,2,1,0:T(8,128)}) fusion(bf16[1,2,640,256]{3,2,1,0:T(8,128)(2,1)S(1)} %copy-done.2, f32[2,640,256]{2,1,0:T(8,128)S(1)} %get-tuple-element.11, f32[1,2,640,256]{3,2,1,0:T(8,128)S(1)} %copy-done, f32[1,2,640,256]{3,2,1,0:T(8,128)S(1)} %copy-done.1), kind=kLoop, calls=%fused_computation.5 | loop fusion | flops 5570560 | bytes 7864320 | tf_op jit(solution)/shard_map/convert_element_type | solution.py:34
  101.6 0.0 copy-done.3
  101.6 0.0 copy-done.4
  101.6 0.0 copy-done.5
  101.6 1.5 %fusion.7 = (bf16[1,256,640]{2,1,0:T(8,128)(2,1)}, f32[1,256,640]{2,1,0:T(8,128)}, f32[1,256,640]{2,1,0:T(8,128)}) fusion(bf16[1,256,640]{2,1,0:T(8,128)(2,1)S(1)} %copy-done.5, f32[256,640]{1,0:T(8,128)S(1)} %get-tuple-element.12, f32[1,256,640]{2,1,0:T(8,128)S(1)} %copy-done.3, f32[1,256,640]{2,1,0:T(8,128)S(1)} %copy-done.4), kind=kLoop, calls=%fused_computation.14 | loop fusion | flops 2785280 | bytes 3932160 | tf_op jit(solution)/shard_map/convert_element_type | solution.py:34
  103.1 0.8 copy.18
Async XLA Ops:
  0.6 98.4 %copy-start = (f32[1,2,640,256]{3,2,1,0:T(8,128)S(1)}, f32[1,2,640,256]{3,2,1,0:T(8,128)}, u32[]{:S(2)}) copy-start(f32[1,2,640,256]{3,2,1,0:T(8,128)} %param.16) | copy-start | bytes 3932164
  0.6 98.4 %copy-start.1 = (f32[1,2,640,256]{3,2,1,0:T(8,128)S(1)}, f32[1,2,640,256]{3,2,1,0:T(8,128)}, u32[]{:S(2)}) copy-start(f32[1,2,640,256]{3,2,1,0:T(8,128)} %param.17) | copy-start | bytes 3932164
  0.7 98.4 %copy-start.2 = (bf16[1,2,640,256]{3,2,1,0:T(8,128)(2,1)S(1)}, bf16[1,2,640,256]{3,2,1,0:T(8,128)(2,1)}, u32[]{:S(2)}) copy-start(bf16[1,2,640,256]{3,2,1,0:T(8,128)(2,1)} %param.14) | copy-start | bytes 1966084
  99.0 2.5 %copy-start.3 = (f32[1,256,640]{2,1,0:T(8,128)S(1)}, f32[1,256,640]{2,1,0:T(8,128)}, u32[]{:S(2)}) copy-start(f32[1,256,640]{2,1,0:T(8,128)} %param.18) | copy-start | bytes 1966084
  99.1 2.5 %copy-start.4 = (f32[1,256,640]{2,1,0:T(8,128)S(1)}, f32[1,256,640]{2,1,0:T(8,128)}, u32[]{:S(2)}) copy-start(f32[1,256,640]{2,1,0:T(8,128)} %param.19) | copy-start | bytes 1966084
  99.1 2.5 %copy-start.5 = (bf16[1,256,640]{2,1,0:T(8,128)(2,1)S(1)}, bf16[1,256,640]{2,1,0:T(8,128)(2,1)}, u32[]{:S(2)}) copy-start(bf16[1,256,640]{2,1,0:T(8,128)(2,1)} %param.15) | copy-start | bytes 983044

commit v2 on v1

--- a/solution.py
+++ b/solution.py
@@ -372,19 +372,21 @@
             zbuf[rows_of(h), at : at + kz] = both.reshape(batch, kz).astype(jnp.bfloat16)
         z_copy(h).start()
 
-    each = -(-ny // max(1, last - 1))
+    def pass_some(h, piece):
+        for ry in range(ny):
+            at = min(ry, 2 * last - 1)
+
+            @pl.when(h * 2 + piece == at)
+            def _(ry=ry):
+                pass_pair(last, ry)
 
     def step(h, carry):
         spread, act = activations(h)
+        pass_some(h, 0)
         for owner in range(4):
             gacc[owner * part : (owner + 1) * part] = weight_grad(h, owner, spread)
         project(h, act)
-        for ry in range(ny):
-
-            @pl.when(h == ry // each)
-            def _(ry=ry):
-                pass_pair(last, ry)
-
+        pass_some(h, 1)
         return carry
 
     lax.fori_loop(0, last, step, 0)
@@ -476,6 +478,11 @@
         ).astype(jnp.bfloat16)
         grad_sends[4 + k].start()
 
+    for k, came, hf in ((3, from_r, 0), (2, from_l, 1)):
+        arrived(came.at[hf], rwait.at[k])
+        cols = slice(hf * wide, (hf + 1) * wide)
+        gacc[own_rows(g), cols] = gacc[own_rows(g), cols] + came[hf].astype(jnp.float32)
+
     arrived(orecv, owait)
     for side in range(2):
         done = jnp.zeros((rows_t, lanes), jnp.float32)
@@ -488,14 +495,10 @@
         out[:, side * lanes : (side + 1) * lanes] = done.astype(jnp.bfloat16)
 
     totals = []
-    for first, second, hf in ((4, 3, 0), (2, 5, 1)):
-        arrived(from_l.at[hf], rwait.at[first])
-        arrived(from_r.at[hf], rwait.at[second])
-        totals.append(
-            gacc[own_rows(g), hf * wide : (hf + 1) * wide]
-            + from_l[hf].astype(jnp.float32)
-            + from_r[hf].astype(jnp.float32)
-        )
+    for k, came, hf in ((4, from_l, 0), (5, from_r, 1)):
+        arrived(came.at[hf], rwait.at[k])
+        cols = slice(hf * wide, (hf + 1) * wide)
+        totals.append(gacc[own_rows(g), cols] + came[hf].astype(jnp.float32))
     gpair[0] = totals[0][:, :hid]
     gpair[1, :, : hid // 2] = totals[0][:, hid:]
     gpair[1, :, hid // 2 :] = totals[1][:, : hid // 2]
@@ -595,6 +598,59 @@
     )
 
 
+def update_kernel(*refs):
+    ins, outs, scratch, sem = refs[:9], refs[9:16], refs[16:22], refs[22]
+    copies = [pltpu.make_async_copy(ins[8], outs[6], sem.at[0])]
+    copies[0].start()
+    for which in range(2):
+        weight, gradient, first, second = ins[which * 4 : which * 4 + 4]
+        kept, to = scratch[which * 3 : which * 3 + 3], outs[which * 3 : which * 3 + 3]
+        rows = weight.shape[0]
+        count = 8 if which == 0 else 4
+        size = rows // count
+        for at in range(0, rows, size):
+            piece = slice(at, at + size)
+            made = adamw_update(
+                weight[piece], gradient[piece], first[piece], second[piece]
+            )
+            for value, keep, end in zip(made, kept, to, strict=True):
+                keep[piece] = value
+                copies.append(
+                    pltpu.make_async_copy(
+                        keep.at[pl.ds(at, size)],
+                        end.at[pl.ds(at, size)],
+                        sem.at[len(copies)],
+                    )
+                )
+                copies[-1].start()
+    for copy in copies:
+        copy.wait()
+
+
+def update(pair, down, layer_out):
+    vmem = pl.BlockSpec(memory_space=pltpu.VMEM)
+    hbm = pl.BlockSpec(memory_space=pltpu.HBM)
+    kinds = []
+    for group in (pair, down):
+        for dtype in (jnp.bfloat16, jnp.float32, jnp.float32):
+            kinds.append((group[0].shape, dtype))
+    return pl.pallas_call(
+        update_kernel,
+        out_shape=tuple(
+            jax.ShapeDtypeStruct(*kind)
+            for kind in (*kinds, (layer_out.shape, layer_out.dtype))
+        ),
+        in_specs=[vmem] * 9,
+        out_specs=(hbm,) * 7,
+        scratch_shapes=[pltpu.VMEM(*kind) for kind in kinds]
+        + [pltpu.SemaphoreType.DMA((37,))],
+        compiler_params=pltpu.CompilerParams(vmem_limit_bytes=32 * 1024 * 1024),
+        cost_estimate=pl.CostEstimate(
+            flops=15_000_000, bytes_accessed=12_000_000, transcendentals=1_000_000
+        ),
+    )(*pair, *down, layer_out)
+
+
 def body(
     tokens,
     cotangent,
@@ -610,20 +666,23 @@
     layer_out, own_pair, own_down = experts_step(
         tokens, cotangent, expert_ids, gate_weights, gate_up[0], down_proj[0]
     )
-    gate_up_new, gate_up_first_new, gate_up_second_new = adamw_update(
-        gate_up, own_pair[None], gate_up_first, gate_up_second
-    )
-    down_new, down_first_new, down_second_new = adamw_update(
-        down_proj, own_down[None], down_first, down_second
-    )
+
+    def flat(a):
+        return a.reshape(-1, a.shape[-1])
+
+    pair = [flat(a) for a in (gate_up, own_pair, gate_up_first, gate_up_second)]
+    down = [flat(a) for a in (down_proj, own_down, down_first, down_second)]
+    made = update(pair, down, layer_out)
+    pair_new = [a.reshape(gate_up.shape) for a in made[:3]]
+    down_new = [a.reshape(down_proj.shape) for a in made[3:6]]
     return (
-        layer_out,
-        gate_up_new,
-        down_new,
-        gate_up_first_new,
-        gate_up_second_new,
-        down_first_new,
-        down_second_new,
+        made[6],
+        pair_new[0],
+        down_new[0],
+        pair_new[1],
+        pair_new[2],
+        down_new[1],
+        down_new[2],
     )
 
 

time: 104 us -> 102 us (0.981)
  other arithmetic: 4.04 us -> 0 us
  Pallas kernels: 98.3 us -> 101 us
    convert_element_type x2 -> x0, other arithmetic: 4.04 us -> none  [adamw_update(): return (updated.astype(jnp.bfloat16), first_new, second_new)]
    pallas_call x0 -> x1, Pallas kernels: none -> 2.74 us  [update(): pl.pallas_call(update_kernel, out_shape=tuple((jax.ShapeDtypeStruct(*kind...]
where the time goes in v2:
time: 102 us
  Pallas kernels  101 us (99%)
    pallas_call x1, Pallas kernels, experts_step(): pl.pallas_call(functools.partial(moe_kernel, ny, nz), out_shape=(jax.Shap...  98.2 us
    pallas_call x1, Pallas kernels, update(): pl.pallas_call(update_kernel, out_shape=tuple((jax.ShapeDtypeStruct(*kind...  2.74 us

profile of v2, /device:TPU:32, one launch (start us, length us, event | category | flops | bytes accessed | tf_op | source)
XLA Modules:
  0.0 101.7 jit_solution(15187256191131736276)
XLA Ops:
  0.6 0.0 copy-start
  0.6 0.0 copy-start.1
  0.7 0.0 copy-start.2
  0.7 0.0 copy-start.3
  0.7 0.0 copy-start.4
  0.7 0.0 copy-start.5
  0.7 98.2 %shard_map.153 = (bf16[128,2560]{1,0:T(8,128)(2,1)S(1)}, f32[2,640,256]{2,1,0:T(8,128)S(1)}, f32[256,640]{1,0:T(8,128)S(1)}) custom-call(bf16[128,2560]{1,0:T(8,128)(2,1)} %tokens_in.1, bf16[128,2560]{1,0:T(8,128)(2,1)} %cot_in.1, s32[6,128]{1,0:T(8,128)} %bitcast.31, f32[6,128]{1,0:T(8,128)} %bitcast.32, bf16[2,640,256]{2,1,0:T(8,128)(2,1)} %bitcast.19, ...), custom_call_target="tpu_custom_call" | custom-call | flops 8000000000 | bytes 10000000 | tf_op jit(solution)/shard_map/pallas_call | solution.py:532
  98.9 0.0 copy-done
  98.9 0.0 copy-done.1
  98.9 0.0 copy-done.2
  98.9 0.0 copy-done.3
  98.9 0.0 copy-done.4
  99.0 0.0 copy-done.5
  99.0 2.7 %shard_map.154 = (bf16[1280,256]{1,0:T(8,128)(2,1)}, f32[1280,256]{1,0:T(8,128)}, f32[1280,256]{1,0:T(8,128)}, bf16[256,640]{1,0:T(8,128)(2,1)}, f32[256,640]{1,...) custom-call(bf16[1280,256]{1,0:T(8,128)(2,1)S(1)} %bitcast.20, f32[1280,256]{1,0:T(8,128)S(1)} %bitcast.18, ...), custom_call_target="tpu_custom_call" | custom-call | flops 15000000 | bytes 12000000 | tf_op jit(solution)/shard_map/pallas_call | solution.py:637
Async XLA Ops:
  0.6 98.3 %copy-start = (f32[1,2,640,256]{3,2,1,0:T(8,128)S(1)}, f32[1,2,640,256]{3,2,1,0:T(8,128)}, u32[]{:S(2)}) copy-start(f32[1,2,640,256]{3,2,1,0:T(8,128)} %param.16) | copy-start | bytes 3932164
  0.6 98.3 %copy-start.1 = (f32[1,2,640,256]{3,2,1,0:T(8,128)S(1)}, f32[1,2,640,256]{3,2,1,0:T(8,128)}, u32[]{:S(2)}) copy-start(f32[1,2,640,256]{3,2,1,0:T(8,128)} %param.17) | copy-start | bytes 3932164
  0.7 98.3 %copy-start.2 = (bf16[1,2,640,256]{3,2,1,0:T(8,128)(2,1)S(1)}, bf16[1,2,640,256]{3,2,1,0:T(8,128)(2,1)}, u32[]{:S(2)}) copy-start(bf16[1,2,640,256]{3,2,1,0:T(8,128)(2,1)} %param.14) | copy-start | bytes 1966084
  0.7 98.3 %copy-start.3 = (f32[1,256,640]{2,1,0:T(8,128)S(1)}, f32[1,256,640]{2,1,0:T(8,128)}, u32[]{:S(2)}) copy-start(f32[1,256,640]{2,1,0:T(8,128)} %param.18) | copy-start | bytes 1966084
  0.7 98.3 %copy-start.4 = (f32[1,256,640]{2,1,0:T(8,128)S(1)}, f32[1,256,640]{2,1,0:T(8,128)}, u32[]{:S(2)}) copy-start(f32[1,256,640]{2,1,0:T(8,128)} %param.19) | copy-start | bytes 1966084
  0.7 98.3 %copy-start.5 = (bf16[1,256,640]{2,1,0:T(8,128)(2,1)S(1)}, bf16[1,256,640]{2,1,0:T(8,128)(2,1)}, u32[]{:S(2)}) copy-start(bf16[1,256,640]{2,1,0:T(8,128)(2,1)} %param.15) | copy-start | bytes 983044

commit v3 on v2

--- a/solution.py
+++ b/solution.py
@@ -406,21 +406,30 @@
             device_id_type=MESH,
         )
 
+    def piece_of(n):
+        return pl.ds(n * half, half)
+
     grad_sends = [
-        grad_copy(0, gs.at[0, 0], part_l, right),
-        grad_copy(1, gs.at[0, 1], part_r, left),
-        grad_copy(2, gs.at[1, 1], from_l.at[1], right),
-        grad_copy(3, gs.at[2, 0], from_r.at[0], left),
-        grad_copy(4, gs.at[1, 0], from_l.at[0], right),
-        grad_copy(5, gs.at[2, 1], from_r.at[1], left),
+        grad_copy(0, gs.at[0, 0, piece_of(0)], part_l.at[piece_of(0)], right),
+        grad_copy(1, gs.at[0, 0, piece_of(1)], part_l.at[piece_of(1)], right),
+        grad_copy(2, gs.at[0, 1, piece_of(0)], part_r.at[piece_of(0)], left),
+        grad_copy(3, gs.at[0, 1, piece_of(1)], part_r.at[piece_of(1)], left),
+        grad_copy(4, gs.at[1, 1], from_l.at[1], right),
+        grad_copy(5, gs.at[2, 0], from_r.at[0], left),
+        grad_copy(6, gs.at[1, 0, piece_of(0)], from_l.at[0, piece_of(0)], right),
+        grad_copy(7, gs.at[1, 0, piece_of(1)], from_l.at[0, piece_of(1)], right),
+        grad_copy(8, gs.at[2, 1, piece_of(0)], from_r.at[1, piece_of(0)], left),
+        grad_copy(9, gs.at[2, 1, piece_of(1)], from_r.at[1, piece_of(1)], left),
     ]
     spread, act = activations(last)
     wide = gacc.shape[1] // 2
-    for slot, owner, sent in ((0, g_opp, ((0, 0), (1, 1))), (1, g_right, ((2, 1),)), (2, g_left, ((3, 0),))):
+    for slot, owner, sent in ((0, g_opp, ((0, 0), (2, 1))), (1, g_right, ((4, 1),)), (2, g_left, ((5, 0),))):
         full = weight_grad(last, owner, spread)
         for k, hf in sent:
             gs[slot, hf] = full[:, hf * wide : (hf + 1) * wide].astype(jnp.bfloat16)
             grad_sends[k].start()
+            if not slot:
+                grad_sends[k + 1].start()
         if slot:
             hf = 1 - sent[0][1]
             gacc[own_rows(owner), hf * wide : (hf + 1) * wide] = full[
@@ -468,17 +477,20 @@
     gacc[own_rows(g)] = weight_grad(last, g, spread)
     send_back(last)
 
-    for k, (came, slot, hf, owner) in enumerate(
-        ((part_l, 1, 0, g_right), (part_r, 2, 1, g_left))
-    ):
-        arrived(came, rwait.at[k])
-        gs[slot, hf] = (
-            gacc[own_rows(owner), hf * wide : (hf + 1) * wide]
-            + came[...].astype(jnp.float32)
-        ).astype(jnp.bfloat16)
-        grad_sends[4 + k].start()
-
-    for k, came, hf in ((3, from_r, 0), (2, from_l, 1)):
+    for n in range(2):
+        for k, came, slot, hf, owner in (
+            (0, part_l, 1, 0, g_right),
+            (2, part_r, 2, 1, g_left),
+        ):
+            arrived(came.at[piece_of(n)], rwait.at[k + n])
+            rows = pl.ds(pl.multiple_of(owner * part + n * half, 64), half)
+            gs[slot, hf, n * half : (n + 1) * half] = (
+                gacc[rows, hf * wide : (hf + 1) * wide]
+                + came[n * half : (n + 1) * half].astype(jnp.float32)
+            ).astype(jnp.bfloat16)
+            grad_sends[6 + k + n].start()
+
+    for k, came, hf in ((5, from_r, 0), (4, from_l, 1)):
         arrived(came.at[hf], rwait.at[k])
         cols = slice(hf * wide, (hf + 1) * wide)
         gacc[own_rows(g), cols] = gacc[own_rows(g), cols] + came[hf].astype(jnp.float32)
@@ -495,8 +507,9 @@
         out[:, side * lanes : (side + 1) * lanes] = done.astype(jnp.bfloat16)
 
     totals = []
-    for k, came, hf in ((4, from_l, 0), (5, from_r, 1)):
-        arrived(came.at[hf], rwait.at[k])
+    for k, came, hf in ((6, from_l, 0), (8, from_r, 1)):
+        for n in range(2):
+            arrived(came.at[hf, piece_of(n)], rwait.at[k + n])
         cols = slice(hf * wide, (hf + 1) * wide)
         totals.append(gacc[own_rows(g), cols] + came[hf].astype(jnp.float32))
     gpair[0] = totals[0][:, :hid]
@@ -571,8 +584,8 @@
             dma((nh,)),
             dma,
             dma,
-            dma((6,)),
-            dma((6,)),
+            dma((10,)),
+            dma((10,)),
             dma((4,)),
         ],
         compiler_params=pltpu.CompilerParams(

time: 102 us -> 102 us (level)
  no operation moved by 1% of the time
where the time goes in v3:
time: 102 us
  Pallas kernels  101 us (99%)
    pallas_call x1, Pallas kernels, experts_step(): pl.pallas_call(functools.partial(moe_kernel, ny, nz), out_shape=(jax.Shap...  98.3 us
    pallas_call x1, Pallas kernels, update(): pl.pallas_call(update_kernel, out_shape=tuple((jax.ShapeDtypeStruct(*kind...  2.74 us

profile of v3, /device:TPU:32, one launch (start us, length us, event | category | flops | bytes accessed | tf_op | source)
XLA Modules:
  0.0 101.8 jit_solution(14309094381176562677)
XLA Ops:
  0.6 0.0 copy-start
  0.6 0.0 copy-start.1
  0.7 0.0 copy-start.2
  0.7 0.0 copy-start.3
  0.7 0.0 copy-start.4
  0.7 0.0 copy-start.5
  0.7 98.3 %shard_map.153 = (bf16[128,2560]{1,0:T(8,128)(2,1)S(1)}, f32[2,640,256]{2,1,0:T(8,128)S(1)}, f32[256,640]{1,0:T(8,128)S(1)}) custom-call(bf16[128,2560]{1,0:T(8,128)(2,1)} %tokens_in.1, bf16[128,2560]{1,0:T(8,128)(2,1)} %cot_in.1, s32[6,128]{1,0:T(8,128)} %bitcast.31, f32[6,128]{1,0:T(8,128)} %bitcast.32, bf16[2,640,256]{2,1,0:T(8,128)(2,1)} %bitcast.19, ...), custom_call_target="tpu_custom_call" | custom-call | flops 8000000000 | bytes 10000000 | tf_op jit(solution)/shard_map/pallas_call | solution.py:545
  99.0 0.0 copy-done
  99.0 0.0 copy-done.1
  99.0 0.0 copy-done.2
  99.0 0.0 copy-done.3
  99.0 0.0 copy-done.4
  99.0 0.0 copy-done.5
  99.1 2.7 %shard_map.154 = (bf16[1280,256]{1,0:T(8,128)(2,1)}, f32[1280,256]{1,0:T(8,128)}, f32[1280,256]{1,0:T(8,128)}, bf16[256,640]{1,0:T(8,128)(2,1)}, f32[256,640]{1,...) custom-call(bf16[1280,256]{1,0:T(8,128)(2,1)S(1)} %bitcast.20, f32[1280,256]{1,0:T(8,128)S(1)} %bitcast.18, ...), custom_call_target="tpu_custom_call" | custom-call | flops 15000000 | bytes 12000000 | tf_op jit(solution)/shard_map/pallas_call | solution.py:650
Async XLA Ops:
  0.6 98.4 %copy-start = (f32[1,2,640,256]{3,2,1,0:T(8,128)S(1)}, f32[1,2,640,256]{3,2,1,0:T(8,128)}, u32[]{:S(2)}) copy-start(f32[1,2,640,256]{3,2,1,0:T(8,128)} %param.16) | copy-start | bytes 3932164
  0.6 98.4 %copy-start.1 = (f32[1,2,640,256]{3,2,1,0:T(8,128)S(1)}, f32[1,2,640,256]{3,2,1,0:T(8,128)}, u32[]{:S(2)}) copy-start(f32[1,2,640,256]{3,2,1,0:T(8,128)} %param.17) | copy-start | bytes 3932164
  0.7 98.4 %copy-start.2 = (bf16[1,2,640,256]{3,2,1,0:T(8,128)(2,1)S(1)}, bf16[1,2,640,256]{3,2,1,0:T(8,128)(2,1)}, u32[]{:S(2)}) copy-start(bf16[1,2,640,256]{3,2,1,0:T(8,128)(2,1)} %param.14) | copy-start | bytes 1966084
  0.7 98.4 %copy-start.3 = (f32[1,256,640]{2,1,0:T(8,128)S(1)}, f32[1,256,640]{2,1,0:T(8,128)}, u32[]{:S(2)}) copy-start(f32[1,256,640]{2,1,0:T(8,128)} %param.18) | copy-start | bytes 1966084
  0.7 98.4 %copy-start.4 = (f32[1,256,640]{2,1,0:T(8,128)S(1)}, f32[1,256,640]{2,1,0:T(8,128)}, u32[]{:S(2)}) copy-start(f32[1,256,640]{2,1,0:T(8,128)} %param.19) | copy-start | bytes 1966084
  0.7 98.4 %copy-start.5 = (bf16[1,256,640]{2,1,0:T(8,128)(2,1)S(1)}, bf16[1,256,640]{2,1,0:T(8,128)(2,1)}, u32[]{:S(2)}) copy-start(bf16[1,256,640]{2,1,0:T(8,128)(2,1)} %param.15) | copy-start | bytes 983044
